TPU v7x, 32 devices: a whole 2x2x4 slice. The times are simulated.
32 devices in a mesh: gx: 16 (over z, x, core), gz: 2 (over y).
Axes of the slice: x: 2, y: 2, z: 4, core: 2. Of those that a mesh axis runs over, the one named last changes fastest.
Arguments:
- velocity: float32 [2, 2, 1, 4096, 2048], P(None, None, None, 'gx', 'gz'), may hold values from -6 to 6
- previous: float32 [2, 2, 1, 4096, 2048], P(None, None, None, 'gx', 'gz'), may hold values from -12 to 12
- base_flow: float32 [1], replicated, may hold values from -1 to 1
Outputs:
- velocity_next: float32 [2, 2, 1, 4096, 2048], P(None, None, None, 'gx', 'gz')
- nonlinear: float32 [2, 2, 1, 4096, 2048], P(None, None, None, 'gx', 'gz')
All inputs are finite; a program needn't handle non-finite values.
Results may differ from a plain program's by a relative error of at most 0.00014.
Values sent between devices are 32-bit elements; how exact they have to be, the bound alone decides.
A program may use at most 128 MiB of HBM per device.

v0:
```python
import math

import jax
import jax.numpy as jnp
from jax import lax
from jax.sharding import PartitionSpec as P

NX = 4096
NZ = 2048


TWO_PI = 2.0 * math.pi
VISCOSITY = 0.05
TIME_STEP = 0.2
GAMMA_NEW = 8.0 / 15.0
ZETA_OLD = -17.0 / 60.0


def partner_2(x, axis, distance):
    return lax.ppermute(x, axis, [(i, i ^ 1 << distance) for i in range(lax.axis_size(axis))])


def exact_einsum(pattern, left_array, right_array):
    return jnp.einsum(
        pattern,
        left_array,
        right_array,
        precision=lax.Precision.HIGHEST,
        preferred_element_type=jnp.float32,
    )


def phase_table(left_ints, right_ints, period, direction):
    phase_angle = (
        direction * TWO_PI / period * (left_ints * right_ints % period).astype(jnp.float32)
    )
    return (jnp.cos(phase_angle), jnp.sin(phase_angle))


def complex_apply(value_real, value_imag, table_real, table_imag, pattern):
    out_real = exact_einsum(pattern, value_real, table_real) - exact_einsum(
        pattern, value_imag, table_imag
    )
    out_imag = exact_einsum(pattern, value_real, table_imag) + exact_einsum(
        pattern, value_imag, table_real
    )
    return (out_real, out_imag)


def residue_of(position, levels):
    reversed_bits = jnp.zeros((), jnp.int32)
    for level in range(levels):
        reversed_bits = reversed_bits + ((position >> level & 1) << levels - 1 - level)
    return reversed_bits


def section_twiddle(position, half_span):
    phase_angle = TWO_PI / (2 * half_span) * (position % half_span).astype(jnp.float32)
    return (jnp.cos(phase_angle), jnp.sin(phase_angle))


def spread_butterfly(values):
    position = lax.axis_index("gx")
    levels = lax.axis_size("gx").bit_length() - 1
    for level in reversed(range(levels)):
        half_span = 1 << level
        partner = partner_2(values, "gx", level)
        upper_half = position >> level & 1 == 1
        cosine, sine_part = section_twiddle(position, half_span)
        difference = partner - values
        rotated = jnp.stack(
            [
                difference[:, 0] * cosine - difference[:, 1] * sine_part,
                difference[:, 0] * sine_part + difference[:, 1] * cosine,
            ],
            axis=1,
        )
        values = jnp.where(upper_half, rotated, values + partner)
    return (values, residue_of(position, levels))


def gather_butterfly(values):
    position = lax.axis_index("gx")
    levels = lax.axis_size("gx").bit_length() - 1
    for level in range(levels):
        half_span = 1 << level
        partner = partner_2(values, "gx", level)
        upper_half = position >> level & 1 == 1
        cosine, sine_part = section_twiddle(position, half_span)
        upper_item = jnp.where(upper_half, values, partner)
        lower_item = jnp.where(upper_half, partner, values)
        turned = jnp.stack(
            [
                upper_item[:, 0] * cosine + upper_item[:, 1] * sine_part,
                upper_item[:, 1] * cosine - upper_item[:, 0] * sine_part,
            ],
            axis=1,
        )
        values = jnp.where(upper_half, lower_item - turned, lower_item + turned)
    return values


def axial_table(residue, mode_count, device_count):
    numbers = jnp.arange(mode_count, dtype=jnp.int32)
    points = residue + device_count * numbers
    cosine, sine_part = phase_table(points[:, None], numbers[None, :], NX, 1.0)
    norm_scale = 1.0 / math.sqrt(NX)
    return (cosine * norm_scale, sine_part * norm_scale)


def span_table(groups, span_size):
    residues = jnp.arange(groups, dtype=jnp.int32)[:, None, None]
    grid_rows = jnp.arange(span_size, dtype=jnp.int32)[None, :, None]
    mode_cols = jnp.arange(span_size, dtype=jnp.int32)[None, None, :]
    cosine, sine_part = phase_table(mode_cols, residues + groups * grid_rows, NZ, 1.0)
    norm_scale = 1.0 / math.sqrt(NZ)
    return (cosine * norm_scale, sine_part * norm_scale)


def spanwise_work(received):
    fields, pair_size, planes, row_count, extent = received.shape
    groups = lax.axis_size("gz")
    span_size = extent // groups
    blocks = received.reshape(fields, pair_size, planes, row_count, groups, span_size)
    group_ids = jnp.arange(groups, dtype=jnp.int32)
    mix_real, mix_imag = phase_table(group_ids[:, None], group_ids[None, :], groups, 1.0)
    section_real, section_imag = complex_apply(
        blocks[:, 0], blocks[:, 1], mix_real, mix_imag, "fylcj,rc->fylrj"
    )
    table_real, table_imag = span_table(groups, span_size)
    physical = exact_einsum("fylrj,rtj->fylrt", section_real, table_real) - exact_einsum(
        "fylrj,rtj->fylrt", section_imag, table_imag
    )
    products = jnp.stack(
        [physical[0] * physical[0], physical[0] * physical[1], physical[1] * physical[1]]
    )
    back_real = exact_einsum("pylrt,rtj->pylrj", products, table_real)
    back_imag = -exact_einsum("pylrt,rtj->pylrj", products, table_imag)
    out_real, out_imag = complex_apply(back_real, back_imag, mix_real, -mix_imag, "pylrj,cr->pylcj")
    spectra = jnp.stack([out_real, out_imag], axis=1)
    return spectra.reshape(3, pair_size, planes, row_count, extent)


def span_round(values, work):
    span_spectra = work(lax.all_to_all(values, "gz", split_axis=3, concat_axis=4, tiled=True))
    return lax.all_to_all(span_spectra, "gz", split_axis=4, concat_axis=3, tiled=True)


def signed_block(start, mode_count, extent):
    numbers = start + jnp.arange(mode_count, dtype=jnp.int32)
    return jnp.where(2 * numbers < extent, numbers, numbers - extent)


def local(velocity, previous, base_flow):
    mode_count = velocity.shape[3]
    span_size = velocity.shape[4]
    device_count = lax.axis_size("gx")
    spread, residue = spread_butterfly(velocity)
    table_real, table_imag = axial_table(residue, mode_count, device_count)
    along_real, along_imag = complex_apply(
        spread[:, 0], spread[:, 1], table_real, table_imag, "fymq,sm->fysq"
    )
    physical_along = jnp.stack([along_real, along_imag], axis=1)
    returned = span_round(physical_along, spanwise_work)
    local_real, local_imag = complex_apply(
        returned[:, 0], returned[:, 1], table_real.T, -table_imag.T, "fysq,ms->fymq"
    )
    local_spectra = jnp.stack([local_real, local_imag], axis=1)
    product_spectra = gather_butterfly(local_spectra)
    modes_along = signed_block(lax.axis_index("gx") * mode_count, mode_count, NX)
    modes_across = signed_block(lax.axis_index("gz") * span_size, span_size, NZ)
    wave_along = (modes_along.astype(jnp.float32) * (TWO_PI / NX))[:, None]
    wave_across = (modes_across.astype(jnp.float32) * (TWO_PI / NZ))[None, :]
    keep = jnp.logical_and(
        (3 * jnp.abs(modes_along) < NX)[:, None], (3 * jnp.abs(modes_across) < NZ)[None, :]
    ).astype(jnp.float32)
    shear = base_flow[:, None, None] * wave_along[None]
    prod_real = product_spectra[:, 0]
    prod_imag = product_spectra[:, 1]
    first_real = (
        keep * (wave_along * prod_imag[0] + wave_across * prod_imag[1]) + shear * velocity[0, 1]
    )
    first_imag = (
        -keep * (wave_along * prod_real[0] + wave_across * prod_real[1]) - shear * velocity[0, 0]
    )
    second_real = (
        keep * (wave_along * prod_imag[1] + wave_across * prod_imag[2]) + shear * velocity[1, 1]
    )
    second_imag = (
        -keep * (wave_along * prod_real[1] + wave_across * prod_real[2]) - shear * velocity[1, 0]
    )
    nonlinear = jnp.stack(
        [jnp.stack([first_real, first_imag]), jnp.stack([second_real, second_imag])]
    )
    damping = jnp.exp(-VISCOSITY * (wave_along * wave_along + wave_across * wave_across))
    advanced = damping * (velocity + TIME_STEP * (GAMMA_NEW * nonlinear + ZETA_OLD * previous))
    return (advanced, nonlinear)


def solution(mesh):
    in_specs = (P(None, None, None, "gx", "gz"), P(None, None, None, "gx", "gz"), P())
    out_specs = (P(None, None, None, "gx", "gz"), P(None, None, None, "gx", "gz"))
    return jax.shard_map(local, mesh=mesh, in_specs=in_specs, out_specs=out_specs, check_vma=False)
```

profile of v0, /device:TPU:9, one launch (start us, length us, event | category | flops | bytes accessed | tf_op | source)
XLA Modules:
  0.0 1541.7 jit_solution(14843414121054455125)
XLA Ops:
  0.6 4.8 copy.116
  7.9 180.2 %collective-permute-done = f32[2,2,1,256,1024]{4,3,0,2,1:T(8,128)} collective-permute-done((f32[2,2,1,256,1024]{4,3,0,2,1:T(8,128)}, f32[2,2,1,256,1024]{4,3,0,2,1:T(8,128)}, u32[]{:S(2)}, u32[]{:S(2)}) %collective-permute-start) | collective-permute-done | bytes 4194336 | tf_op jit(solution)/shard_map/ppermute | solution.py:20
  188.1 4.4 copy_subtract_fusion
  194.7 5.7 maximum_select_fusion
  200.9 91.5 %collective-permute-done.1 = f32[2,2,1,256,1024]{4,3,0,2,1:T(8,128)} collective-permute-done((f32[2,2,1,256,1024]{4,3,0,2,1:T(8,128)}, f32[2,2,1,256,1024]{4,3,0,2,1:T(8,128)}, u32[]{:S(2)}, u32[]{:S(2)}) %collective-permute-start.1) | collective-permute-done | bytes 4194336 | tf_op jit(solution)/shard_map/ppermute | solution.py:20
  292.4 4.4 sub.151
  297.4 7.0 maximum_select_fusion.1
  305.8 89.7 %collective-permute-done.2 = f32[2,2,1,256,1024]{4,3,0,2,1:T(8,128)} collective-permute-done((f32[2,2,1,256,1024]{4,3,0,2,1:T(8,128)}, f32[2,2,1,256,1024]{4,3,0,2,1:T(8,128)}, u32[]{:S(2)}, u32[]{:S(2)}) %collective-permute-start.2) | collective-permute-done | bytes 4194336 | tf_op jit(solution)/shard_map/ppermute | solution.py:20
  395.4 4.4 sub.153
  400.4 7.0 maximum_select_fusion.2
  409.7 7.1 collective-permute-done.3
  416.8 4.4 sub.155
  421.7 5.2 maximum_select_fusion.3
  435.7 14.4 add_bitcast_fusion.3
  450.6 5.2 copy.123
  455.8 5.6 all-to-all-start
  461.5 47.1 %all-to-all-done = f32[2,2,1,256,1024]{4,0,2,1,3:T(2,128)} async-done(((f32[2,2,1,256,1024]{4,0,2,1,3:T(2,128)}), f32[2,2,1,256,1024]{4,0,2,1,3:T(2,128)}, u32[]{:S(2)}, u32[]{:S(2)}) %all-to-all-start) | async-done | bytes 4194336 | tf_op jit(solution)/shard_map/all_to_all | solution.py:145
  508.6 5.4 copy.196
  514.0 7.8 fusion.44
  521.8 7.8 fusion.43
  529.6 8.6 subtract_bitcast_fusion.3
  538.2 8.4 add_bitcast_fusion.2
  546.6 45.0 %fusion.5 = f32[2,1024,2,128]{3,1,2,0:T(8,128)S(1)} fusion(s32[2,1024]{1,0:T(2,128)S(1)} %iota_add_fusion, f32[2,128,2,1024]{3,2,1,0:T(2,128)S(1)} %add_bitcast_fusion.2), kind=kOutput, calls=%fused_computation.8 | convolution fusion | flops 6473908224 | bytes 4202496 | tf_op jit(solution)/shard_map/fylrj,rtj->fylrt/dot_general | solution.py:24
  591.7 44.8 %subtract_bitcast_fusion.2 = f32[2,1,128,2,1024]{2,4,0,3,1:T(8,128)S(1)} fusion(f32[2,1024,2,128]{3,1,2,0:T(8,128)S(1)} %fusion.5, f32[2,128,2,1024]{3,2,1,0:T(2,128)S(1)} %subtract_bitcast_fusion.3, s32[2,1024]{1,0:T(2,128)S(1)} %iota_add_fusion), kind=kOutput, calls=%fused_computation.79 | convolution fusion | flops 6474432512 | bytes 6299648 | tf_op jit(solution)/shard_map/fylrj,rtj->fylrt/dot_general | solution.py:24
  638.7 51.9 %fusion.38 = f32[3,128,2,1024]{1,3,0,2:T(8,128)} fusion(s32[2,1024]{1,0:T(2,128)S(1)} %iota_add_fusion, f32[3,128,2,1024]{1,3,0,2:T(8,128)S(1)} %maximum_bitcast_fusion.16), kind=kOutput, calls=%fused_computation.96 | convolution fusion | flops 9695133696 | bytes 6299648 | tf_op jit(solution)/shard_map/pylrt,rtj->pylrj/dot_general | solution.py:24
  694.8 12.5 fusion.124
  707.4 12.9 fusion.118
  720.3 51.6 %negate_bitcast_fusion = f32[3,128,2,1024]{1,3,0,2:T(8,128)} fusion(s32[2,1024]{1,0:T(2,128)S(1)} %iota_add_fusion, f32[3,128,2,1024]{1,3,0,2:T(8,128)S(1)} %copy-done.5), kind=kOutput, calls=%fused_computation.62 | convolution fusion | flops 9695920128 | bytes 6299648 | tf_op jit(solution)/shard_map/pylrt,rtj->pylrj/dot_general | solution.py:24
  777.7 14.2 subtract_bitcast_fusion.1
  791.9 4.4 stack.100
  796.4 5.4 copy.136
  801.8 15.0 add_bitcast_fusion.1
  816.8 4.3 stack.101
  821.1 5.3 copy.137
  826.4 7.5 pad_maximum_fusion
  834.0 72.7 %all_to_all.33 = f32[3,2,1,128,2048]{3,1,2,0,4:T(2,128)} all-to-all(f32[3,2,1,128,2048]{3,1,2,0,4:T(2,128)S(1)} %pad_maximum_fusion), channel_id=1, replica_groups=mesh['gx'=16,'gz'=2] {'gz'}, dimensions={4} | all-to-all | bytes 12582912 | tf_op jit(solution)/shard_map/all_to_all | solution.py:146
  906.6 10.4 copy.138
  917.1 6.0 fusion.29
  931.4 4.5 add_bitcast_fusion
  938.6 9.8 collective-permute-done.4
  954.9 135.7 %collective-permute-done.5 = f32[3,2,1,256,1024]{4,3,0,2,1:T(8,128)} collective-permute-done((f32[3,2,1,256,1024]{4,3,0,2,1:T(8,128)S(1)}, f32[3,2,1,256,1024]{4,3,0,2,1:T(8,128)}, u32[]{:S(2)}, u32[]{:S(2)}) %collective-permute-start.5) | collective-permute-done | bytes 6291488 | tf_op jit(solution)/shard_map/ppermute | solution.py:20
  1090.6 5.0 broadcast_select_fusion.1
  1099.2 6.9 add_select_fusion.3
  1106.1 135.8 %collective-permute-done.6 = f32[3,2,1,256,1024]{4,3,0,2,1:T(8,128)S(1)} collective-permute-done((f32[3,2,1,256,1024]{4,3,0,2,1:T(8,128)S(1)}, f32[3,2,1,256,1024]{4,3,0,2,1:T(8,128)S(1)}, u32[]{:S(2)}, u32[]{:S(2)}) %collective-permute-start.6) | collective-permute-done | bytes 6291488 | tf_op jit(solution)/shard_map/ppermute | solution.py:20
  1253.0 269.4 %collective-permute-done.7 = f32[3,2,1,256,1024]{4,3,0,2,1:T(8,128)} collective-permute-done((f32[3,2,1,256,1024]{4,3,0,2,1:T(8,128)}, f32[3,2,1,256,1024]{4,3,0,2,1:T(8,128)}, u32[]{:S(2)}, u32[]{:S(2)}) %collective-permute-start.7) | collective-permute-done | bytes 6291488 | tf_op jit(solution)/shard_map/ppermute | solution.py:20
  1522.4 4.3 broadcast_select_fusion.3
  1527.6 4.6 add_select_fusion.1
  1534.2 7.3 fusion.27
  (60 shorter events, 66.0 us)
Async XLA Ops:
  5.4 182.7 %collective-permute-start = (f32[2,2,1,256,1024]{4,3,0,2,1:T(8,128)}, f32[2,2,1,256,1024]{4,3,0,2,1:T(8,128)}, u32[]{:S(2)}, u32[]{:S(2)}) collective-permute-start(f32[2,2,1,256,1024]{4,3,0,2,1:T(8,128)} %copy.116), channel_id=1, source_target_pairs={{0,16},{2,18},{4,20},{6,22},{8,24},{10,26},{12,28},{14,30},{16,0},... | collective-permute-start | bytes 12582920 | tf_op jit(solution)/shard_map/ppermute | solution.py:20
  192.5 2.2 copy-start
  200.4 92.0 %collective-permute-start.1 = (f32[2,2,1,256,1024]{4,3,0,2,1:T(8,128)}, f32[2,2,1,256,1024]{4,3,0,2,1:T(8,128)}, u32[]{:S(2)}, u32[]{:S(2)}) collective-permute-start(f32[2,2,1,256,1024]{4,3,0,2,1:T(8,128)} %maximum_select_fusion), channel_id=1, source_target_pairs={{0,8},{2,10},{4,12},{6,14},{8,0},{10,2},{12,4},{14,6},{16,24},{18,... | collective-permute-start | bytes 12582920 | tf_op jit(solution)/shard_map/ppermute | solution.py:20
  304.4 91.0 %collective-permute-start.2 = (f32[2,2,1,256,1024]{4,3,0,2,1:T(8,128)}, f32[2,2,1,256,1024]{4,3,0,2,1:T(8,128)}, u32[]{:S(2)}, u32[]{:S(2)}) collective-permute-start(f32[2,2,1,256,1024]{4,3,0,2,1:T(8,128)} %maximum_select_fusion.1), channel_id=1, source_target_pairs={{0,4},{2,6},{4,0},{6,2},{8,12},{10,14},{12,8},{14,10},{16,20},{18,... | collective-permute-start | bytes 12582920 | tf_op jit(solution)/shard_map/ppermute | solution.py:20
  407.4 9.4 collective-permute-start.3
  455.8 52.8 %all-to-all-start = ((f32[2,2,1,256,1024]{4,0,2,1,3:T(2,128)}), f32[2,2,1,256,1024]{4,0,2,1,3:T(2,128)}, u32[]{:S(2)}, u32[]{:S(2)}) async-start(f32[2,2,1,256,1024]{4,0,2,1,3:T(2,128)} %copy.123), calls=%async_computation | async-start | bytes 8388608 | tf_op jit(solution)/shard_map/all_to_all | solution.py:145
  707.4 12.9 copy-start.5
  776.1 1.7 copy-start.6
  917.1 6.0 copy-start.2
  936.5 12.0 collective-permute-start.4
  951.4 139.2 %copy-start.3 = (f32[3,1,1,256,1024]{4,3,0,2,1:T(8,128)}, f32[3,1,1,256,1024]{4,3,0,2,1:T(8,128)S(1)}, u32[]{:S(2)}) copy-start(f32[3,1,1,256,1024]{4,3,0,2,1:T(8,128)S(1)} %get-tuple-element.19) | copy-start | bytes 9437188
  951.4 139.2 %copy-start.4 = (f32[3,1,1,256,1024]{4,3,0,2,1:T(8,128)}, f32[3,1,1,256,1024]{4,3,0,2,1:T(8,128)S(1)}, u32[]{:S(2)}) copy-start(f32[3,1,1,256,1024]{4,3,0,2,1:T(8,128)S(1)} %get-tuple-element.20) | copy-start | bytes 9437188
  953.7 136.9 %collective-permute-start.5 = (f32[3,2,1,256,1024]{4,3,0,2,1:T(8,128)S(1)}, f32[3,2,1,256,1024]{4,3,0,2,1:T(8,128)}, u32[]{:S(2)}, u32[]{:S(2)}) collective-permute-start(f32[3,2,1,256,1024]{4,3,0,2,1:T(8,128)S(1)} %add_select_fusion.4), channel_id=1, source_target_pairs={{0,4},{2,6},{4,0},{6,2},{8,12},{10,14},{12,8},{14,10},{16,20},{18,... | collective-permute-start | bytes 18874376 | tf_op jit(solution)/shard_map/ppermute | solution.py:20
  1106.1 135.9 %collective-permute-start.6 = (f32[3,2,1,256,1024]{4,3,0,2,1:T(8,128)S(1)}, f32[3,2,1,256,1024]{4,3,0,2,1:T(8,128)S(1)}, u32[]{:S(2)}, u32[]{:S(2)}) collective-permute-start(f32[3,2,1,256,1024]{4,3,0,2,1:T(8,128)S(1)} %add_select_fusion.3), channel_id=1, source_target_pairs={{0,8},{2,10},{4,12},{6,14},{8,0},{10,2},{12,4},{14,6},{16,24},{18,... | collective-permute-start | bytes 18874376 | tf_op jit(solution)/shard_map/ppermute | solution.py:20
  1249.0 273.4 %collective-permute-start.7 = (f32[3,2,1,256,1024]{4,3,0,2,1:T(8,128)}, f32[3,2,1,256,1024]{4,3,0,2,1:T(8,128)}, u32[]{:S(2)}, u32[]{:S(2)}) collective-permute-start(f32[3,2,1,256,1024]{4,3,0,2,1:T(8,128)} %add_select_fusion.2), channel_id=1, source_target_pairs={{0,16},{2,18},{4,20},{6,22},{8,24},{10,26},{12,28},{14,30},{16,0},... | collective-permute-start | bytes 18874376 | tf_op jit(solution)/shard_map/ppermute | solution.py:20
  1527.6 4.6 copy-start.1
where the time goes:
time: 1550 us; the launch traced here: 1540 us
  waiting for transfers between devices  966 us (62%)
  matrix products  322 us (21%)
  other arithmetic  103 us (7%)
  blocking collectives  72.7 us (5%)
  local copies, waits for them, and re-layouts  57 us (4%)
  starting transfers between devices  18.2 us (1%)
    ppermute x8, waiting for transfers between devices, partner_2(): lax.ppermute(x, axis, [(i, i ^ 1 << distance) for i in range(lax.axis_siz...  919 us
    dot_general x20, matrix products, exact_einsum(): jnp.einsum(pattern, left_array, right_array, precision=lax.Precision.HIGH...  322 us
    all_to_all x1, blocking collectives, span_round(): lax.all_to_all(span_spectra, 'gz', split_axis=4, concat_axis=3, tiled=True)  72.7 us
    all_to_all x1, waiting for transfers between devices, span_round(): lax.all_to_all(values, 'gz', split_axis=3, concat_axis=4, tiled=True)  47.1 us
  transfers between devices with their start and end apart: 9, of which 9 were waited for; matrix products, arithmetic and copies ran while one was open for 0% of the time, Pallas kernels for 0%

commit v1 on v0

--- a/solution.py
+++ b/solution.py
@@ -2,7 +2,10 @@
 
 import jax
 import jax.numpy as jnp
+import numpy as np
 from jax import lax
+from jax.experimental import pallas as pl
+from jax.experimental.pallas import tpu as pltpu
 from jax.sharding import PartitionSpec as P
 
 NX = 4096
@@ -197,7 +200,353 @@
     return (advanced, nonlinear)
 
 
+XR = 16
+XS = NX // XR
+ZR = 8
+ZS = NZ // ZR
+LOW = (0, 1, 2)
+HIGH = (5, 6, 7)
+MIB = 1 << 20
+
+
+def split_table(table):
+    high = table.astype(np.float32).astype(jnp.bfloat16)
+    low = (table - high.astype(np.float64)).astype(np.float32).astype(jnp.bfloat16)
+    return high, low
+
+
+def z_table():
+    r = np.arange(ZR)[:, None, None]
+    b = np.arange(ZS)[None, :, None]
+    s = np.arange(ZS)[None, None, :]
+    angle = TWO_PI / NZ * ((b * (r + ZR * s)) % NZ)
+    cos, sin = np.cos(angle) / math.sqrt(NZ), np.sin(angle) / math.sqrt(NZ)
+    top = np.concatenate([cos, sin], axis=2)
+    bottom = np.concatenate([-sin, cos], axis=2)
+    return split_table(np.concatenate([top, bottom], axis=1))
+
+
+def x_table():
+    r = np.arange(XR)[:, None, None]
+    s = np.arange(XS)[None, :, None]
+    m = np.arange(XS)[None, None, :]
+    angle = TWO_PI / NX * ((m * (r + XR * s)) % NX)
+    cos, sin = np.cos(angle) / math.sqrt(NX), np.sin(angle) / math.sqrt(NX)
+    return split_table(np.concatenate([cos, -sin], axis=2))
+
+
+def turn(value, numerator, size, sign):
+    re, im = value
+    numerator = numerator % size
+    if numerator == 0:
+        return re, im
+    if 4 * numerator == size:
+        return (-im, re) if sign > 0 else (im, -re)
+    if 8 * numerator == size:
+        h = math.sqrt(0.5)
+        return ((re - im) * h, (re + im) * h) if sign > 0 else ((re + im) * h, (im - re) * h)
+    if 8 * numerator == 3 * size:
+        h = math.sqrt(0.5)
+        return ((-re - im) * h, (re - im) * h) if sign > 0 else ((im - re) * h, (-re - im) * h)
+    c = math.cos(TWO_PI * numerator / size)
+    s = sign * math.sin(TWO_PI * numerator / size)
+    return re * c - im * s, re * s + im * c
+
+
+def small_dft(values, sign):
+    size = len(values)
+    if size == 1:
+        return values
+    even = small_dft(values[0::2], sign)
+    odd = small_dft(values[1::2], sign)
+    half = size // 2
+    out = [None] * size
+    for i in range(half):
+        re, im = turn(odd[i], i, size, sign)
+        out[i] = (even[i][0] + re, even[i][1] + im)
+        out[i + half] = (even[i][0] - re, even[i][1] - im)
+    return out
+
+
+def parts_of(value):
+    high = value.astype(jnp.bfloat16)
+    return high, (value - high.astype(jnp.float32)).astype(jnp.bfloat16)
+
+
+def dot3(a_high, a_low, b_high, b_low, dims):
+    def dot(a, b):
+        return lax.dot_general(a, b, (dims, ((), ())), preferred_element_type=jnp.float32)
+
+    return dot(a_high, b_high) + (dot(a_high, b_low) + dot(a_low, b_high))
+
+
+def merge(first, second, low_half):
+    return (
+        jnp.where(low_half, first, pltpu.roll(second, 64, 1)),
+        jnp.where(low_half, pltpu.roll(first, 64, 1), second),
+    )
+
+
+def z_inverse_kernel(v_ref, high_ref, low_ref, out_ref, th_ref, tl_ref):
+    rows = v_ref.shape[3]
+    step = 16
+    for c in range(2):
+        def body(i, carry):
+            at = pl.multiple_of(i * step, step)
+            for lane in range(0, ZS, 128):
+                values = [
+                    tuple(
+                        v_ref[c, p, a // 4, pl.ds(at, step), pl.ds((a % 4) * ZS + lane, 128)]
+                        for p in range(2)
+                    )
+                    for a in range(ZR)
+                ]
+                for r, pair in enumerate(small_dft(values, 1)):
+                    for p in range(2):
+                        high, low = parts_of(pair[p])
+                        th_ref[r, pl.ds(c * rows + at, step), pl.ds(p * ZS + lane, 128)] = high
+                        tl_ref[r, pl.ds(c * rows + at, step), pl.ds(p * ZS + lane, 128)] = low
+            return carry
+        lax.fori_loop(0, rows // step, body, 0)
+
+    def group(r, carry):
+        done = dot3(th_ref[r], tl_ref[r], high_ref[r], low_ref[r], ((1,), (0,)))
+        low_half = lax.broadcasted_iota(jnp.int32, (rows, 128), 1) < 64
+        for p in range(2):
+            for t in range(2):
+                at = p * ZS + t * 128
+                even, odd = merge(done[:rows, at : at + 128], done[rows:, at : at + 128], low_half)
+                out_ref[r, 2 * t, p] = even
+                out_ref[r, 2 * t + 1, p] = odd
+        return carry
+    lax.fori_loop(0, ZR, group, 0)
+
+
+def x_kernel(v_ref, ih_ref, il_ref, fh_ref, fl_ref, out_ref, th_ref, tl_ref, u_ref):
+    rows = v_ref.shape[3]
+    step = 16
+    for r in range(2):
+        def body(i, carry):
+            at = pl.multiple_of(i * step, step)
+            values = [
+                tuple(v_ref[g, r, p, pl.ds(at, step), :] for p in range(2)) for g in range(XR)
+            ]
+            for res, pair in enumerate(small_dft(values, 1)):
+                for p in range(2):
+                    high, low = parts_of(pair[p])
+                    th_ref[res, pl.ds(p * XS + r * rows + at, step), :] = high
+                    tl_ref[res, pl.ds(p * XS + r * rows + at, step), :] = low
+            return carry
+        lax.fori_loop(0, rows // step, body, 0)
+
+    def residue(res, carry):
+        field = dot3(ih_ref[res], il_ref[res], th_ref[res], tl_ref[res], ((1,), (0,)))
+        swapped = pltpu.roll(field, 64, 1)
+        products = jnp.concatenate([field * field, field * swapped], axis=1)
+        high, low = parts_of(products)
+        u_ref[res] = dot3(fh_ref[res], fl_ref[res], high, low, ((1,), (0,)))
+        return carry
+    lax.fori_loop(0, XR, residue, 0)
+
+    low_half = lax.broadcasted_iota(jnp.int32, (8, 128), 1) < 64
+    for r in range(2):
+        def back(i, carry):
+            at = pl.multiple_of(i * 8, 8)
+            for h in range(2):
+                values = [
+                    tuple(
+                        u_ref[res, pl.ds(p * XS + r * rows + at, 8), pl.ds(h * 128, 128)]
+                        for p in range(2)
+                    )
+                    for res in range(XR)
+                ]
+                for g, (re, im) in enumerate(small_dft(values, -1)):
+                    if h == 0:
+                        out_ref[g, r, 0, pl.ds(at, 8), :] = re
+                        out_ref[g, r, 1, pl.ds(at, 8), :] = im
+                    else:
+                        out_ref[g, r, 2, pl.ds(at, 8), :] = jnp.where(low_half, re, im)
+            return carry
+        lax.fori_loop(0, rows // 8, back, 0)
+
+
+def z_forward_kernel(v_ref, high_ref, low_ref, wave_ref, keep_ref, out_ref, w_ref):
+    rows = v_ref.shape[3]
+    low_half = lax.broadcasted_iota(jnp.int32, (rows, 128), 1) < 64
+
+    def group(r, carry):
+        real, imag, mixed = ([v_ref[r, j, x] for j in range(4)] for x in range(3))
+        p0r, p2r, p0i, p2i, p1r, p1i = [], [], [], [], [], []
+        for source, first, second in ((real, p0r, p2r), (imag, p0i, p2i), (mixed, p1r, p1i)):
+            for t in range(2):
+                a, b = merge(source[2 * t], source[2 * t + 1], low_half)
+                first.append(a)
+                second.append(b)
+        lines = jnp.concatenate(
+            [jnp.concatenate(x, axis=1) for x in (p0r + p0i, p1r + p1i, p2r + p2i)], axis=0
+        )
+        high, low = parts_of(lines)
+        w_ref[r] = dot3(high, low, high_ref[r], low_ref[r], ((1,), (1,)))
+        return carry
+    lax.fori_loop(0, ZR, group, 0)
+
+    def body(i, carry):
+        at = pl.multiple_of(i * 8, 8)
+        wave_along = wave_ref[pl.ds(at, 8), :]
+        keep_along = keep_ref[pl.ds(at, 8), :]
+        for lane in range(0, ZS, 128):
+            spectra = []
+            for j in range(3):
+                values = [
+                    tuple(
+                        w_ref[r, pl.ds(j * rows + at, 8), pl.ds(p * ZS + lane, 128)]
+                        for p in range(2)
+                    )
+                    for r in range(ZR)
+                ]
+                spectra.append(small_dft(values, -1))
+            for half, groups in enumerate((LOW, HIGH)):
+                for place, a in enumerate(groups):
+                    start = a * ZS + lane - (NZ if half else 0)
+                    mode = start + lax.broadcasted_iota(jnp.int32, (8, 128), 1)
+                    wave_across = mode.astype(jnp.float32) * (TWO_PI / NZ)
+                    keep = jnp.where(3 * jnp.abs(mode) < NZ, keep_along, 0.0)
+                    (ar, ai), (br, bi), (cr, ci) = (x[a] for x in spectra)
+                    to = (pl.ds(at, 8), pl.ds(place * ZS + lane, 128))
+                    out_ref[(half, 0) + to] = keep * (wave_along * ai + wave_across * bi)
+                    out_ref[(half, 1) + to] = -keep * (wave_along * ar + wave_across * br)
+                    out_ref[(half, 2) + to] = keep * (wave_along * bi + wave_across * ci)
+                    out_ref[(half, 3) + to] = -keep * (wave_along * br + wave_across * cr)
+        return carry
+    lax.fori_loop(0, rows // 8, body, 0)
+
+
+def advance_kernel(half_ref, base_ref, v_ref, old_ref, term_ref, along_ref, across_ref, next_ref, non_ref):
+    rows, extent = v_ref.shape[2:]
+    wave_along = along_ref[:, :1]
+    wave_across = across_ref[:1, :]
+    damping = jnp.exp(-VISCOSITY * (wave_along * wave_along + wave_across * wave_across))
+    shear = base_ref[0] * wave_along
+    empty = jnp.zeros((rows, extent - term_ref.shape[3]), jnp.float32)
+    for c in range(2):
+        for p in range(2):
+            term = term_ref[0, 2 * c + p]
+            term = jnp.where(
+                half_ref[0] == 0,
+                jnp.concatenate([term, empty], axis=1),
+                jnp.concatenate([empty, term], axis=1),
+            )
+            other = shear * v_ref[c, 1 - p]
+            result = term + other if p == 0 else term - other
+            non_ref[c, p] = result
+            next_ref[c, p] = damping * (
+                v_ref[c, p] + TIME_STEP * (GAMMA_NEW * result + ZETA_OLD * old_ref[c, p])
+            )
+
+
+def whole(*_):
+    return pl.BlockSpec(memory_space=pltpu.VMEM)
+
+
+def params(limit):
+    return pltpu.CompilerParams(vmem_limit_bytes=limit * MIB)
+
+
+def lines_local(velocity, previous, base_flow):
+    velocity, previous = velocity[:, :, 0], previous[:, :, 0]
+    mode_count, extent = velocity.shape[2:]
+    rows = mode_count // 2
+    gx, gz = lax.axis_index("gx"), lax.axis_index("gz")
+    f32, bf16 = jnp.float32, jnp.bfloat16
+    zh, zl = z_table()
+    xh, xl = x_table()
+    fh, fl = np.swapaxes(xh, 1, 2), np.swapaxes(xl, 1, 2)
+
+    lines = lax.all_to_all(
+        velocity.reshape(2, 2, 2, rows, extent), "gz", split_axis=2, concat_axis=2, tiled=True
+    )
+    along_z = pl.pallas_call(
+        z_inverse_kernel,
+        out_shape=jax.ShapeDtypeStruct((ZR, 4, 2, rows, 128), f32),
+        in_specs=[whole()] * 3,
+        out_specs=whole(),
+        scratch_shapes=[pltpu.VMEM((ZR, 2 * rows, 2 * ZS), bf16)] * 2,
+        compiler_params=params(48),
+        name="z_inverse",
+    )(lines, zh, zl)
+    swapped = exchange(along_z.reshape(32, 2, rows, 128))
+    worked = pl.pallas_call(
+        x_kernel,
+        out_shape=jax.ShapeDtypeStruct((XR, 2, 3, rows, 128), f32),
+        in_specs=[whole()] * 5,
+        out_specs=whole(),
+        scratch_shapes=[pltpu.VMEM((XR, 2 * XS, 128), bf16)] * 2
+        + [pltpu.VMEM((XR, 2 * XS, 256), f32)],
+        compiler_params=params(56),
+        name="x_work",
+    )(swapped.reshape(XR, 2, 2, rows, 128), xh, xl, fh, fl)
+    returned = exchange(worked.reshape(32, 3, rows, 128))
+
+    def modes(start, count, size):
+        numbers = start + jnp.arange(count, dtype=jnp.int32)
+        return jnp.where(2 * numbers < size, numbers, numbers - size)
+
+    own = modes(gx * mode_count + gz * rows, rows, NX)[:, None]
+    own_wave = jnp.broadcast_to(own.astype(f32) * (TWO_PI / NX), (rows, 128))
+    own_keep = jnp.broadcast_to((3 * jnp.abs(own) < NX).astype(f32), (rows, 128))
+    active = len(LOW) * ZS
+    terms = pl.pallas_call(
+        z_forward_kernel,
+        out_shape=jax.ShapeDtypeStruct((2, 4, rows, active), f32),
+        in_specs=[whole()] * 5,
+        out_specs=whole(),
+        scratch_shapes=[pltpu.VMEM((ZR, 3 * rows, 2 * ZS), f32)],
+        compiler_params=params(48),
+        name="z_forward",
+    )(returned.reshape(ZR, 4, 3, rows, 128), zh, zl, own_wave, own_keep)
+    terms = lax.all_to_all(terms, "gz", split_axis=0, concat_axis=0, tiled=True)
+
+    along = modes(gx * mode_count, mode_count, NX).astype(f32) * (TWO_PI / NX)
+    across = modes(gz * extent, extent, NZ).astype(f32) * (TWO_PI / NZ)
+    block = 64
+    per = rows // block
+    scalar = pl.BlockSpec(memory_space=pltpu.SMEM)
+    field = pl.BlockSpec((2, 2, block, extent), lambda i: (0, 0, i, 0))
+    advanced, nonlinear = pl.pallas_call(
+        advance_kernel,
+        grid=(mode_count // block,),
+        out_shape=[jax.ShapeDtypeStruct(velocity.shape, f32)] * 2,
+        in_specs=[
+            scalar,
+            scalar,
+            field,
+            field,
+            pl.BlockSpec((1, 4, block, active), lambda i: (i // per, 0, i % per, 0)),
+            pl.BlockSpec((block, 128), lambda i: (i, 0)),
+            pl.BlockSpec((8, extent), lambda i: (0, 0)),
+        ],
+        out_specs=[field, field],
+        compiler_params=params(48),
+        name="advance",
+    )(
+        gz.astype(jnp.int32)[None],
+        base_flow,
+        velocity,
+        previous,
+        terms,
+        jnp.broadcast_to(along[:, None], (mode_count, 128)),
+        jnp.broadcast_to(across[None], (8, extent)),
+    )
+    return advanced[:, :, None], nonlinear[:, :, None]
+
+
+def exchange(value):
+    return lax.all_to_all(value, ("gx", "gz"), split_axis=0, concat_axis=0, tiled=True)
+
+
 def solution(mesh):
     in_specs = (P(None, None, None, "gx", "gz"), P(None, None, None, "gx", "gz"), P())
     out_specs = (P(None, None, None, "gx", "gz"), P(None, None, None, "gx", "gz"))
-    return jax.shard_map(local, mesh=mesh, in_specs=in_specs, out_specs=out_specs, check_vma=False)
+    fits = mesh.shape["gx"] == XR and mesh.shape["gz"] == 2
+    work = lines_local if fits else local
+    return jax.shard_map(work, mesh=mesh, in_specs=in_specs, out_specs=out_specs, check_vma=False)

time: 1550 us -> 403 us (0.26)
  waiting for transfers between devices: 966 us -> 172 us
  matrix products: 322 us -> 0 us
  other arithmetic: 103 us -> 0.04 us
  blocking collectives: 72.7 us -> 149 us
  Pallas kernels: 0 us -> 61 us
  local copies, waits for them, and re-layouts: 57 us -> 6.72 us
    ppermute x8 -> x0, waiting for transfers between devices: 919 us -> none  [partner_2(): lax.ppermute(x, axis, [(i, i ^ 1 << distance) for i in range(lax.axis_siz...]
    dot_general x20 -> x0, matrix products: 322 us -> none  [exact_einsum(): jnp.einsum(pattern, left_array, right_array, precision=lax.Precision.HIGH...]
    all_to_all x1 -> x2, waiting for transfers between devices: 47.1 us -> 172 us  [the longest x1 137 us: exchange(): lax.all_to_all(value, ('gx', 'gz'), split_axis=0, concat_axis=0, tiled=True)]
    all_to_all x1 -> x2, blocking collectives: 72.7 us -> 149 us  [the longest x1 99.8 us: exchange(): lax.all_to_all(value, ('gx', 'gz'), split_axis=0, concat_axis=0, tiled=True)]
    pallas_call x0 -> x4, Pallas kernels: none -> 61 us  [the longest x1 28 us: lines_local(): pl.pallas_call(x_kernel, out_shape=jax.ShapeDtypeStruct((XR, 2, 3, rows,...]
    select_n x12 -> x0, other arithmetic: 56.3 us -> none  [the longest x4 25 us: spread_butterfly(): values = jnp.where(upper_half, rotated, values + partner)]
    another operation x7 -> x1, local copies, waits for them, and re-layouts: 33.1 us -> 2.5 us  [lines_local(): velocity.reshape(2, 2, 2, rows, extent)]
    sub x9 -> x0, other arithmetic: 20.2 us -> none  [the longest x4 17.6 us: spread_butterfly(): difference = partner - values]
  transfers between devices with their start and end apart: 9 -> 2, of which waited for: 9 -> 2; matrix products, arithmetic and copies ran while one was open for 0% -> 0% of each run, Pallas kernels for 0% -> 0%
where the time goes in v1:
time: 403 us; the launch traced here: 399 us
  waiting for transfers between devices  172 us (43%)
  blocking collectives  149 us (37%)
  Pallas kernels  61 us (15%)
  starting transfers between devices  7.77 us (2%)
  local copies, waits for them, and re-layouts  6.72 us (2%)
    all_to_all x1, waiting for transfers between devices, exchange(): lax.all_to_all(value, ('gx', 'gz'), split_axis=0, concat_axis=0, tiled=True)  137 us
    all_to_all x1, blocking collectives, exchange(): lax.all_to_all(value, ('gx', 'gz'), split_axis=0, concat_axis=0, tiled=True)  99.8 us
    all_to_all x1, blocking collectives, lines_local(): lax.all_to_all(velocity.reshape(2, 2, 2, rows, extent), 'gz', split_axis=...  49.4 us
    all_to_all x1, waiting for transfers between devices, lines_local(): terms = lax.all_to_all(terms, 'gz', split_axis=0, concat_axis=0, tiled=True)  35.3 us
    pallas_call x1, Pallas kernels, lines_local(): pl.pallas_call(x_kernel, out_shape=jax.ShapeDtypeStruct((XR, 2, 3, rows,...  28 us
    pallas_call x1, Pallas kernels, lines_local(): pl.pallas_call(z_forward_kernel, out_shape=jax.ShapeDtypeStruct((2, 4, ro...  13.4 us
    pallas_call x1, Pallas kernels, lines_local(): pl.pallas_call(z_inverse_kernel, out_shape=jax.ShapeDtypeStruct((ZR, 4, 2...  11.6 us
  transfers between devices with their start and end apart: 2, of which 2 were waited for; matrix products, arithmetic and copies ran while one was open for 0% of the time, Pallas kernels for 0%

profile of v1, /device:TPU:9, one launch (start us, length us, event | category | flops | bytes accessed | tf_op | source)
XLA Modules:
  0.0 398.5 jit_solution(8526152801061270328)
XLA Ops:
  0.6 2.5 copy.16
  3.1 49.4 %all_to_all.20 = f32[2,2,2,128,1024]{4,3,1,0,2:T(8,128)S(1)} all-to-all(f32[2,2,2,128,1024]{4,3,1,0,2:T(8,128)S(1)} %copy.16), channel_id=1, replica_groups=mesh['gx'=16,'gz'=2] {'gz'}, dimensions={2} | all-to-all | bytes 8388608 | tf_op jit(solution)/shard_map/all_to_all | solution.py:465
  52.6 2.3 copy.17.v_ref
  54.9 11.6 %z_inverse.1 = f32[8,4,2,128,128]{4,3,2,1,0:T(8,128)S(1)} custom-call(f32[2,2,2,128,1024]{4,3,2,1,0:T(8,128)} %copy.17.v_ref, bf16[8,512,512]{2,1,0:T(8,128)(2,1)} %constant.48.clone.high_ref, bf16[8,512,512]{2,1,0:T(8,128)(2,1)} %constant.49.clone.low_ref), custom_call_target="tpu_custom_call" | custom-call | tf_op jit(solution)/shard_map/z_inverse/pallas_call | solution.py:468
  66.5 99.8 %all_to_all.21 = f32[32,2,128,128]{3,2,1,0:T(8,128)} all-to-all(f32[32,2,128,128]{3,2,1,0:T(8,128)S(1)} %bitcast.14), channel_id=1, replica_groups=mesh['gx'=16,'gz'=2] {'gx','gz'}, dimensions={0} | all-to-all | bytes 8388608 | tf_op jit(solution)/shard_map/all_to_all | solution.py:544
  166.3 28.0 %x_work.1 = f32[16,2,3,128,128]{4,3,2,1,0:T(8,128)} custom-call(f32[16,2,2,128,128]{4,3,2,1,0:T(8,128)} %bitcast.18, bf16[16,256,512]{2,1,0:T(8,128)(2,1)} %constant.50.clone.ih_ref, bf16[16,256,512]{2,1,0:T(8,128)(2,1)} %constant.51.clone.il_ref, bf16[16,512,256]{2,1,0:T(8,128)(2,1)} %constant.52.clone.fh_ref, bf16[16,512,256]{2,1,0:T(8,128)(2,1)} %constant.53.clone.fl_ref), custom_call_target="tpu_custom_call" | custom-call | tf_op jit(solution)/shard_map/x_work/pallas_call | solution.py:478
  194.3 3.8 all-to-all-start.2
  198.1 137.1 %all-to-all-done.2 = f32[32,3,128,128]{3,2,1,0:T(8,128)} async-done(((f32[32,3,128,128]{3,2,1,0:T(8,128)}), f32[32,3,128,128]{3,2,1,0:T(8,128)}, u32[]{:S(2)}, u32[]{:S(2)}) %all-to-all-start.2) | async-done | bytes 6291488 | tf_op jit(solution)/shard_map/all_to_all | solution.py:544
  335.2 0.1 broadcast_in_dim.15.wave_ref
  335.3 0.1 broadcast_in_dim.16.keep_ref
  335.4 13.4 %z_forward.1 = f32[2,4,128,768]{3,2,1,0:T(8,128)S(1)} custom-call(f32[8,4,3,128,128]{4,3,2,1,0:T(8,128)} %bitcast.7.v_ref, bf16[8,512,512]{2,1,0:T(8,128)(2,1)} %constant.48.clone.high_ref, bf16[8,512,512]{2,1,0:T(8,128)(2,1)} %constant.49.clone.low_ref, f32[128,128]{1,0:T(8,128)S(1)} %broadcast_in_dim.15.wave_ref, f32[128,128]{1,0:T(8,128)S(1)} %broadcast_in_dim.16.keep_ref), custom_call_target="tpu_custom_call" | custom-call | tf_op jit(solution)/shard_map/z_forward/pallas_call | solution.py:498
  348.8 0.0 copy-start
  348.8 1.7 copy-done
  350.4 3.9 all-to-all-start.3
  355.1 35.3 %all-to-all-done.3.term_ref = f32[2,4,128,768]{3,2,1,0:T(8,128)S(1)} async-done(((f32[2,4,128,768]{3,2,1,0:T(8,128)}), f32[2,4,128,768]{3,2,1,0:T(8,128)S(1)}, u32[]{:S(2)}, u32[]{:S(2)}) %all-to-all-start.3) | async-done | bytes 3145760 | tf_op jit(solution)/shard_map/all_to_all | solution.py:507
  390.4 0.1 broadcast_in_dim.17.along_ref
  390.5 8.0 %advance.1 = (f32[2,2,256,1024]{3,2,1,0:T(8,128)}, f32[2,2,256,1024]{3,2,1,0:T(8,128)}) custom-call(s32[1]{0:T(128)} %bitcast.half_ref, f32[1]{0:T(128)S(6)} %copy.20.base_ref, f32[2,2,256,1024]{3,2,1,0:T(8,128)} %bitcast.17, f32[2,2,256,1024]{3,2,1,0:T(8,128)} %bitcast.19, f32[2,4,128,768]{3,2,1,0:T(8,128)S(1)} %all-to-all-done.3.term_ref, ...), custom_call_target="tpu_custom_call" | custom-call | tf_op jit(solution)/shard_map/advance/pallas_call | solution.py:515
  (5 shorter events, 0.0 us)
Async XLA Ops:
  194.3 140.9 %all-to-all-start.2 = ((f32[32,3,128,128]{3,2,1,0:T(8,128)}), f32[32,3,128,128]{3,2,1,0:T(8,128)}, u32[]{:S(2)}, u32[]{:S(2)}) async-start(f32[32,3,128,128]{3,2,1,0:T(8,128)} %bitcast.15), calls=%async_computation.2 | async-start | bytes 12582912 | tf_op jit(solution)/shard_map/all_to_all | solution.py:544
  348.8 1.7 copy-start
  350.4 40.0 %all-to-all-start.3 = ((f32[2,4,128,768]{3,2,1,0:T(8,128)}), f32[2,4,128,768]{3,2,1,0:T(8,128)S(1)}, u32[]{:S(2)}, u32[]{:S(2)}) async-start(f32[2,4,128,768]{3,2,1,0:T(8,128)} %copy-done), calls=%async_computation.3 | async-start | bytes 6291456 | tf_op jit(solution)/shard_map/all_to_all | solution.py:507

commit v2 on v1

--- a/solution.py
+++ b/solution.py
@@ -1,3 +1,4 @@
+import functools
 import math
 
 import jax
@@ -207,6 +208,7 @@
 LOW = (0, 1, 2)
 HIGH = (5, 6, 7)
 MIB = 1 << 20
+PIECES = 2
 
 
 def split_table(table):
@@ -287,20 +289,21 @@
     )
 
 
-def z_inverse_kernel(v_ref, high_ref, low_ref, out_ref, th_ref, tl_ref):
-    rows = v_ref.shape[3]
+def z_inverse_kernel(half_ref, own_ref, other_ref, high_ref, low_ref, out_ref, th_ref, tl_ref):
+    rows = own_ref.shape[2]
     step = 16
+    first = half_ref[0] == 0
     for c in range(2):
         def body(i, carry):
             at = pl.multiple_of(i * step, step)
             for lane in range(0, ZS, 128):
-                values = [
-                    tuple(
-                        v_ref[c, p, a // 4, pl.ds(at, step), pl.ds((a % 4) * ZS + lane, 128)]
-                        for p in range(2)
-                    )
-                    for a in range(ZR)
-                ]
+                values = [None] * ZR
+                for a in range(ZR // 2):
+                    to = (pl.ds(at, step), pl.ds(a * ZS + lane, 128))
+                    own = [own_ref[(c, p) + to] for p in range(2)]
+                    other = [other_ref[(c, p) + to] for p in range(2)]
+                    values[a] = tuple(jnp.where(first, x, y) for x, y in zip(own, other))
+                    values[a + ZR // 2] = tuple(jnp.where(first, y, x) for x, y in zip(own, other))
                 for r, pair in enumerate(small_dft(values, 1)):
                     for p in range(2):
                         high, low = parts_of(pair[p])
@@ -322,10 +325,15 @@
     lax.fori_loop(0, ZR, group, 0)
 
 
-def x_kernel(v_ref, ih_ref, il_ref, fh_ref, fl_ref, out_ref, th_ref, tl_ref, u_ref):
-    rows = v_ref.shape[3]
+def x_kernel(*refs):
+    v_refs, (ih_ref, il_ref, fh_ref, fl_ref) = refs[:PIECES], refs[PIECES : PIECES + 4]
+    out_refs = refs[PIECES + 4 : 2 * PIECES + 4]
+    th_ref, tl_ref, u_ref = refs[2 * PIECES + 4 :]
+    rows = v_refs[0].shape[3]
     step = 16
-    for r in range(2):
+    for r, h in ((r, h) for r in range(2) for h in range(PIECES)):
+        v_ref, base = v_refs[h], (r * PIECES + h) * rows
+
         def body(i, carry):
             at = pl.multiple_of(i * step, step)
             values = [
@@ -334,8 +342,8 @@
             for res, pair in enumerate(small_dft(values, 1)):
                 for p in range(2):
                     high, low = parts_of(pair[p])
-                    th_ref[res, pl.ds(p * XS + r * rows + at, step), :] = high
-                    tl_ref[res, pl.ds(p * XS + r * rows + at, step), :] = low
+                    th_ref[res, pl.ds(p * XS + base + at, step), :] = high
+                    tl_ref[res, pl.ds(p * XS + base + at, step), :] = low
             return carry
         lax.fori_loop(0, rows // step, body, 0)
 
@@ -349,13 +357,15 @@
     lax.fori_loop(0, XR, residue, 0)
 
     low_half = lax.broadcasted_iota(jnp.int32, (8, 128), 1) < 64
-    for r in range(2):
+    for r, n in ((r, n) for r in range(2) for n in range(PIECES)):
+        out_ref, base = out_refs[n], (r * PIECES + n) * rows
+
         def back(i, carry):
             at = pl.multiple_of(i * 8, 8)
             for h in range(2):
                 values = [
                     tuple(
-                        u_ref[res, pl.ds(p * XS + r * rows + at, 8), pl.ds(h * 128, 128)]
+                        u_ref[res, pl.ds(p * XS + base + at, 8), pl.ds(h * 128, 128)]
                         for p in range(2)
                     )
                     for res in range(XR)
@@ -370,7 +380,8 @@
         lax.fori_loop(0, rows // 8, back, 0)
 
 
-def z_forward_kernel(v_ref, high_ref, low_ref, wave_ref, keep_ref, out_ref, w_ref):
+def z_forward_kernel(half_ref, v_ref, high_ref, low_ref, wave_ref, keep_ref, own_ref, other_ref, w_ref):
+    lower = half_ref[0] == 0
     rows = v_ref.shape[3]
     low_half = lax.broadcasted_iota(jnp.int32, (rows, 128), 1) < 64
 
@@ -405,32 +416,49 @@
                     for r in range(ZR)
                 ]
                 spectra.append(small_dft(values, -1))
-            for half, groups in enumerate((LOW, HIGH)):
-                for place, a in enumerate(groups):
+            for place in range(len(LOW)):
+                terms = []
+                for half, groups in enumerate((LOW, HIGH)):
+                    a = groups[place]
                     start = a * ZS + lane - (NZ if half else 0)
                     mode = start + lax.broadcasted_iota(jnp.int32, (8, 128), 1)
                     wave_across = mode.astype(jnp.float32) * (TWO_PI / NZ)
-                    keep = jnp.where(3 * jnp.abs(mode) < NZ, keep_along, 0.0)
+                    keep = jnp.logical_and(3 * jnp.abs(mode) < NZ, keep_along > 0.5)
                     (ar, ai), (br, bi), (cr, ci) = (x[a] for x in spectra)
-                    to = (pl.ds(at, 8), pl.ds(place * ZS + lane, 128))
-                    out_ref[(half, 0) + to] = keep * (wave_along * ai + wave_across * bi)
-                    out_ref[(half, 1) + to] = -keep * (wave_along * ar + wave_across * br)
-                    out_ref[(half, 2) + to] = keep * (wave_along * bi + wave_across * ci)
-                    out_ref[(half, 3) + to] = -keep * (wave_along * br + wave_across * cr)
+                    terms.append(
+                        [
+                            jnp.where(keep, wave_along * ai + wave_across * bi, 0.0),
+                            jnp.where(keep, -(wave_along * ar + wave_across * br), 0.0),
+                            jnp.where(keep, wave_along * bi + wave_across * ci, 0.0),
+                            jnp.where(keep, -(wave_along * br + wave_across * cr), 0.0),
+                        ]
+                    )
+                to = (pl.ds(at, 8), pl.ds(place * ZS + lane, 128))
+                for x in range(4):
+                    own_ref[(x,) + to] = jnp.where(lower, terms[0][x], terms[1][x])
+                    other_ref[(x,) + to] = jnp.where(lower, terms[1][x], terms[0][x])
         return carry
     lax.fori_loop(0, rows // 8, body, 0)
 
 
-def advance_kernel(half_ref, base_ref, v_ref, old_ref, term_ref, along_ref, across_ref, next_ref, non_ref):
+def advance_kernel(half_ref, base_ref, v_ref, old_ref, *refs):
+    own_refs, got_refs = refs[:PIECES], refs[PIECES : 2 * PIECES]
+    along_ref, across_ref, next_ref, non_ref = refs[2 * PIECES :]
+    place = pl.program_id(0)
+    is_own = place // PIECES == half_ref[0]
+    piece = lax.rem(place, PIECES)
     rows, extent = v_ref.shape[2:]
     wave_along = along_ref[:, :1]
     wave_across = across_ref[:1, :]
     damping = jnp.exp(-VISCOSITY * (wave_along * wave_along + wave_across * wave_across))
     shear = base_ref[0] * wave_along
-    empty = jnp.zeros((rows, extent - term_ref.shape[3]), jnp.float32)
+    empty = jnp.zeros((rows, extent - own_refs[0].shape[2]), jnp.float32)
     for c in range(2):
         for p in range(2):
-            term = term_ref[0, 2 * c + p]
+            term = None
+            for h in range(PIECES):
+                this = jnp.where(is_own, own_refs[h][2 * c + p], got_refs[h][2 * c + p])
+                term = this if term is None else jnp.where(piece == h, this, term)
             term = jnp.where(
                 half_ref[0] == 0,
                 jnp.concatenate([term, empty], axis=1),
@@ -452,6 +480,91 @@
     return pltpu.CompilerParams(vmem_limit_bytes=limit * MIB)
 
 
+def kept(block, block_rows):
+    start = block * block_rows
+    return jnp.logical_or(3 * start < NX, 3 * (NX - start - block_rows + 1) < NX)
+
+
+def exchange_kernel(block_rows, src_ref, dst_ref, send_sems, recv_sems, own_sem):
+    across = lax.axis_size("gz")
+    count = lax.axis_size("gx") * across
+    me = lax.axis_index("gx") * across + lax.axis_index("gz")
+
+    def device(t):
+        return (t // across, lax.rem(t, across))
+
+    def wanted(t):
+        return kept(t, block_rows) if block_rows else t >= 0
+
+    barrier = pltpu.get_barrier_semaphore()
+
+    def greet(i, carry):
+        pl.semaphore_signal(
+            barrier,
+            inc=1,
+            device_id=device(lax.rem(me + i, count)),
+            device_id_type=pl.DeviceIdType.MESH,
+        )
+        return carry
+
+    lax.fori_loop(1, count, greet, 0)
+    pl.semaphore_wait(barrier, count - 1)
+
+    def copy(i):
+        t = lax.rem(me + i, count)
+        return pltpu.make_async_remote_copy(
+            src_ref=src_ref.at[t],
+            dst_ref=dst_ref.at[me],
+            send_sem=send_sems.at[i],
+            recv_sem=recv_sems.at[i],
+            device_id=device(t),
+            device_id_type=pl.DeviceIdType.MESH,
+        )
+
+    def start(i, carry):
+        @pl.when(wanted(lax.rem(me + i, count)))
+        def _():
+            copy(i).start()
+
+        return carry
+
+    lax.fori_loop(1, count, start, 0)
+    own = pltpu.make_async_copy(src_ref.at[me], dst_ref.at[me], own_sem)
+    own.start()
+    own.wait()
+
+    def finish(i, carry):
+        @pl.when(wanted(lax.rem(me + i, count)))
+        def _():
+            copy(i).wait_send()
+
+        @pl.when(wanted(me))
+        def _():
+            copy(i).wait_recv()
+
+        return carry
+
+    lax.fori_loop(1, count, finish, 0)
+
+
+def exchange(value, number, block_rows=0):
+    count = value.shape[0]
+    return pl.pallas_call(
+        functools.partial(exchange_kernel, block_rows),
+        out_shape=jax.ShapeDtypeStruct(value.shape, value.dtype),
+        in_specs=[pl.BlockSpec(memory_space=pl.ANY)],
+        out_specs=pl.BlockSpec(memory_space=pl.ANY),
+        scratch_shapes=[
+            pltpu.SemaphoreType.DMA((count,)),
+            pltpu.SemaphoreType.DMA((count,)),
+            pltpu.SemaphoreType.DMA,
+        ],
+        compiler_params=pltpu.CompilerParams(collective_id=number, has_side_effects=True),
+        cost_estimate=pl.CostEstimate(flops=0, bytes_accessed=64 * value.size, transcendentals=0),
+        name="exchange_" + str(number),
+    )(value)
+
+
 def lines_local(velocity, previous, base_flow):
     velocity, previous = velocity[:, :, 0], previous[:, :, 0]
     mode_count, extent = velocity.shape[2:]
@@ -462,30 +575,40 @@
     xh, xl = x_table()
     fh, fl = np.swapaxes(xh, 1, 2), np.swapaxes(xl, 1, 2)
 
-    lines = lax.all_to_all(
-        velocity.reshape(2, 2, 2, rows, extent), "gz", split_axis=2, concat_axis=2, tiled=True
-    )
-    along_z = pl.pallas_call(
-        z_inverse_kernel,
-        out_shape=jax.ShapeDtypeStruct((ZR, 4, 2, rows, 128), f32),
-        in_specs=[whole()] * 3,
-        out_specs=whole(),
-        scratch_shapes=[pltpu.VMEM((ZR, 2 * rows, 2 * ZS), bf16)] * 2,
-        compiler_params=params(48),
-        name="z_inverse",
-    )(lines, zh, zl)
-    swapped = exchange(along_z.reshape(32, 2, rows, 128))
+    piece = rows // PIECES
+    half = gz.astype(jnp.int32)[None]
+    scalar = pl.BlockSpec(memory_space=pltpu.SMEM)
+    swap = [(0, 1), (1, 0)]
+    got, swapped = [], []
+    for h in range(PIECES):
+        part = lax.dynamic_slice_in_dim(velocity, (1 - gz) * rows + h * piece, piece, axis=2)
+        if h:
+            part, got[h - 1] = lax.optimization_barrier((part, got[h - 1]))
+        got.append(lax.ppermute(part, "gz", swap))
+    for h in range(PIECES):
+        mine = lax.dynamic_slice_in_dim(velocity, gz * rows + h * piece, piece, axis=2)
+        if h:
+            mine, swapped[h - 1] = lax.optimization_barrier((mine, swapped[h - 1]))
+        along_z = pl.pallas_call(
+            z_inverse_kernel,
+            out_shape=jax.ShapeDtypeStruct((ZR, 4, 2, piece, 128), f32),
+            in_specs=[scalar] + [whole()] * 4,
+            out_specs=whole(),
+            scratch_shapes=[pltpu.VMEM((ZR, 2 * piece, 2 * ZS), bf16)] * 2,
+            compiler_params=params(40),
+            name="z_inverse",
+        )(half, mine, got[h], zh, zl)
+        swapped.append(exchange(along_z.reshape(32, 2, piece, 128), 1 + h))
     worked = pl.pallas_call(
         x_kernel,
-        out_shape=jax.ShapeDtypeStruct((XR, 2, 3, rows, 128), f32),
-        in_specs=[whole()] * 5,
-        out_specs=whole(),
+        out_shape=[jax.ShapeDtypeStruct((XR, 2, 3, piece, 128), f32)] * PIECES,
+        in_specs=[whole()] * (PIECES + 4),
+        out_specs=[whole()] * PIECES,
         scratch_shapes=[pltpu.VMEM((XR, 2 * XS, 128), bf16)] * 2
         + [pltpu.VMEM((XR, 2 * XS, 256), f32)],
         compiler_params=params(56),
         name="x_work",
-    )(swapped.reshape(XR, 2, 2, rows, 128), xh, xl, fh, fl)
-    returned = exchange(worked.reshape(32, 3, rows, 128))
+    )(*(x.reshape(XR, 2, 2, piece, 128) for x in swapped), xh, xl, fh, fl)
 
     def modes(start, count, size):
         numbers = start + jnp.arange(count, dtype=jnp.int32)
@@ -495,22 +618,28 @@
     own_wave = jnp.broadcast_to(own.astype(f32) * (TWO_PI / NX), (rows, 128))
     own_keep = jnp.broadcast_to((3 * jnp.abs(own) < NX).astype(f32), (rows, 128))
     active = len(LOW) * ZS
-    terms = pl.pallas_call(
-        z_forward_kernel,
-        out_shape=jax.ShapeDtypeStruct((2, 4, rows, active), f32),
-        in_specs=[whole()] * 5,
-        out_specs=whole(),
-        scratch_shapes=[pltpu.VMEM((ZR, 3 * rows, 2 * ZS), f32)],
-        compiler_params=params(48),
-        name="z_forward",
-    )(returned.reshape(ZR, 4, 3, rows, 128), zh, zl, own_wave, own_keep)
-    terms = lax.all_to_all(terms, "gz", split_axis=0, concat_axis=0, tiled=True)
+    own_terms, got_terms = [], []
+    for h in range(PIECES):
+        sent = worked[h].reshape(32, 3, piece, 128)
+        if h:
+            sent, own_terms[h - 1] = lax.optimization_barrier((sent, own_terms[h - 1]))
+        returned = exchange(sent, 1 + PIECES + h, rows)
+        at = slice(h * piece, (h + 1) * piece)
+        mine, other = pl.pallas_call(
+            z_forward_kernel,
+            out_shape=[jax.ShapeDtypeStruct((4, piece, active), f32)] * 2,
+            in_specs=[scalar] + [whole()] * 5,
+            out_specs=[whole()] * 2,
+            scratch_shapes=[pltpu.VMEM((ZR, 3 * piece, 2 * ZS), f32)],
+            compiler_params=params(40),
+            name="z_forward",
+        )(half, returned.reshape(ZR, 4, 3, piece, 128), zh, zl, own_wave[at], own_keep[at])
+        own_terms.append(mine)
+        got_terms.append(lax.ppermute(other, "gz", swap))
 
     along = modes(gx * mode_count, mode_count, NX).astype(f32) * (TWO_PI / NX)
     across = modes(gz * extent, extent, NZ).astype(f32) * (TWO_PI / NZ)
-    block = 64
-    per = rows // block
-    scalar = pl.BlockSpec(memory_space=pltpu.SMEM)
+    block = piece
     field = pl.BlockSpec((2, 2, block, extent), lambda i: (0, 0, i, 0))
     advanced, nonlinear = pl.pallas_call(
         advance_kernel,
@@ -521,7 +650,7 @@
             scalar,
             field,
             field,
-            pl.BlockSpec((1, 4, block, active), lambda i: (i // per, 0, i % per, 0)),
+            *([pl.BlockSpec((4, block, active), lambda i: (0, 0, 0))] * (2 * PIECES)),
             pl.BlockSpec((block, 128), lambda i: (i, 0)),
             pl.BlockSpec((8, extent), lambda i: (0, 0)),
         ],
@@ -529,19 +658,16 @@
         compiler_params=params(48),
         name="advance",
     )(
-        gz.astype(jnp.int32)[None],
+        half,
         base_flow,
         velocity,
         previous,
-        terms,
+        *own_terms,
+        *got_terms,
         jnp.broadcast_to(along[:, None], (mode_count, 128)),
         jnp.broadcast_to(across[None], (8, extent)),
     )
     return advanced[:, :, None], nonlinear[:, :, None]
-
-
-def exchange(value):
-    return lax.all_to_all(value, ("gx", "gz"), split_axis=0, concat_axis=0, tiled=True)
 
 
 def solution(mesh):

time: 403 us -> 360 us (0.89)
  Pallas kernels: 61 us -> 281 us
  blocking collectives: 149 us -> 0 us
  waiting for transfers between devices: 172 us -> 40.8 us
  local copies, waits for them, and re-layouts: 6.72 us -> 30.2 us
    pallas_call x2 -> x7, Pallas kernels: 41.4 us -> 264 us  [the longest x4 221 us: exchange(): pl.pallas_call(functools.partial(exchange_kernel, block_rows), out_shape=...]
    all_to_all x2 -> x0, waiting for transfers between devices: 172 us -> none  [the longest x1 137 us: exchange(): lax.all_to_all(value, ('gx', 'gz'), split_axis=0, concat_axis=0, tiled=True)]
    all_to_all x2 -> x0, blocking collectives: 149 us -> none  [the longest x1 99.8 us: exchange(): lax.all_to_all(value, ('gx', 'gz'), split_axis=0, concat_axis=0, tiled=True)]
    ppermute x0 -> x4, waiting for transfers between devices: none -> 40.8 us  [the longest x2 22.8 us: lines_local(): got.append(lax.ppermute(part, 'gz', swap))]
    unnamed x2 -> x28, local copies, waits for them, and re-layouts: 1.66 us -> 26.1 us
    all_to_all x2 -> x0, starting transfers between devices: 7.77 us -> none  [the longest x1 3.95 us: lines_local(): terms = lax.all_to_all(terms, 'gz', split_axis=0, concat_axis=0, tiled=True)]
    ppermute x0 -> x4, starting transfers between devices: none -> 5.49 us  [the longest x2 3.01 us: lines_local(): got_terms.append(lax.ppermute(other, 'gz', swap))]
    pallas_call x1 -> x2, Pallas kernels: 11.6 us -> 9.06 us  [lines_local(): pl.pallas_call(z_inverse_kernel, out_shape=jax.ShapeDtypeStruct((ZR, 4, 2...]
  transfers between devices with their start and end apart: 2 -> 4, of which waited for: 2 -> 2; matrix products, arithmetic and copies ran while one was open for 0% -> 0% of each run, Pallas kernels for 0% -> 34%
where the time goes in v2:
time: 360 us; the launch traced here: 359 us
  Pallas kernels  281 us (78%)
  waiting for transfers between devices  40.8 us (11%)
  local copies, waits for them, and re-layouts  30.2 us (8%)
  starting transfers between devices  5.49 us (2%)
    pallas_call x4, Pallas kernels, exchange(): pl.pallas_call(functools.partial(exchange_kernel, block_rows), out_shape=...  221 us
    pallas_call x1, Pallas kernels, lines_local(): pl.pallas_call(x_kernel, out_shape=[jax.ShapeDtypeStruct((XR, 2, 3, piece...  27.9 us
    unnamed x28, local copies, waits for them, and re-layouts  26.1 us
    ppermute x2, waiting for transfers between devices, lines_local(): got.append(lax.ppermute(part, 'gz', swap))  22.8 us
    ppermute x2, waiting for transfers between devices, lines_local(): got_terms.append(lax.ppermute(other, 'gz', swap))  18 us
    pallas_call x2, Pallas kernels, lines_local(): pl.pallas_call(z_forward_kernel, out_shape=[jax.ShapeDtypeStruct((4, piec...  14.3 us
    pallas_call x2, Pallas kernels, lines_local(): pl.pallas_call(z_inverse_kernel, out_shape=jax.ShapeDtypeStruct((ZR, 4, 2...  9.06 us
    pallas_call x1, Pallas kernels, lines_local(): pl.pallas_call(advance_kernel, grid=(mode_count // block,), out_shape=[ja...  8.4 us
  transfers between devices with their start and end apart: 4, of which 2 were waited for; matrix products, arithmetic and copies ran while one was open for 0% of the time, Pallas kernels for 34%

profile of v2, /device:TPU:9, one launch (start us, length us, event | category | flops | bytes accessed | tf_op | source)
XLA Modules:
  0.0 359.1 jit_solution(8945424391213889217)
XLA Ops:
  0.6 3.6 dynamic-slice_bitcast_fusion
  4.2 1.2 collective-permute-start
  5.5 22.8 %collective-permute-done.other_ref = f32[2,2,64,1024]{3,2,1,0:T(8,128)S(1)} collective-permute-done((f32[2,2,64,1024]{3,2,1,0:T(8,128)S(1)}, f32[2,2,64,1024]{3,2,1,0:T(8,128)S(1)}, u32[]{:S(2)}, u32[]{:S(2)}) %collective-permute-start) | collective-permute-done | bytes 1048608 | tf_op jit(solution)/shard_map/ppermute | solution.py:587
  28.2 0.0 copy-start.12
  28.2 1.0 copy-done.12
  29.2 1.2 collective-permute-start.1
  30.5 0.1 slice_bitcast_fusion.1
  30.5 0.1 slice_bitcast_fusion
  30.6 0.0 copy-start
  30.6 2.2 copy-done
  32.8 0.0 copy-start.4
  32.8 2.2 copy-done.4
  35.0 0.0 copy-start.13
  35.0 1.2 copy-done.13
  36.2 4.5 %z_inverse.2 = f32[8,4,2,64,128]{4,3,2,1,0:T(8,128)S(1)} custom-call(s32[1]{0:T(128)} %bitcast.half_ref, f32[2,2,64,1024]{3,2,1,0:T(8,128)S(1)} %get-tuple-element.33.own_ref, f32[2,2,64,1024]{3,2,1,0:T(8,128)S(1)} %copy-done.13, bf16[8,512,512]{2,1,0:T(8,128)(2,1)S(1)} %copy-done.4, bf16[8,512,512]{2,1,0:T(8,128)(2,1)S(1)} %copy-done), custom_call_target="tpu_custom_call" | custom-call | tf_op jit(solution)/shard_map/z_inverse/pallas_call | solution.py:592
  40.8 0.0 copy-start.10
  40.8 1.3 copy-done.10
  42.1 50.9 %exchange_1.1 = f32[32,2,64,128]{3,2,1,0:T(8,128)} custom-call(f32[32,2,64,128]{3,2,1,0:T(8,128)} %bitcast.35), custom_call_target="tpu_custom_call" | custom-call | bytes 33554432 | tf_op jit(solution)/shard_map/exchange_1/pallas_call | solution.py:552
  93.0 0.0 collective-permute-done.1.other_ref
  93.0 0.0 copy-start.1
  93.0 2.2 copy-done.1
  95.2 0.0 copy-start.5
  95.2 2.2 copy-done.5
  97.4 4.5 %z_inverse.3 = f32[8,4,2,64,128]{4,3,2,1,0:T(8,128)S(1)} custom-call(s32[1]{0:T(128)} %bitcast.half_ref, f32[2,2,64,1024]{3,2,1,0:T(8,128)S(1)} %get-tuple-element.18.own_ref, f32[2,2,64,1024]{3,2,1,0:T(8,128)S(1)} %collective-permute-done.1.other_ref, bf16[8,512,512]{2,1,0:T(8,128)(2,1)S(1)} %copy-done.5, bf16[8,512,512]{2,1,0:T(8,128)(2,1)S(1)} %copy-done.1), custom_call_target="tpu_custom_call" | custom-call | tf_op jit(solution)/shard_map/z_inverse/pallas_call | solution.py:592
  101.9 0.0 copy-start.11
  102.0 1.3 copy-done.11
  103.3 51.6 %exchange_2.1 = f32[32,2,64,128]{3,2,1,0:T(8,128)} custom-call(f32[32,2,64,128]{3,2,1,0:T(8,128)} %bitcast.36), custom_call_target="tpu_custom_call" | custom-call | bytes 33554432 | tf_op jit(solution)/shard_map/exchange_2/pallas_call | solution.py:552
  154.8 27.9 %x_work.1 = (f32[16,2,3,64,128]{4,3,2,1,0:T(8,128)}, f32[16,2,3,64,128]{4,3,2,1,0:T(8,128)}) custom-call(f32[16,2,2,64,128]{4,3,2,1,0:T(8,128)} %bitcast.38, f32[16,2,2,64,128]{4,3,2,1,0:T(8,128)} %bitcast.39, bf16[16,256,512]{2,1,0:T(8,128)(2,1)} %constant.63.clone.refs_2_, bf16[16,256,512]{2,1,0:T(8,128)(2,1)} %constant.64.clone.refs_3_, ...), custom_call_target="tpu_custom_call" | custom-call | tf_op jit(solution)/shard_map/x_work/pallas_call | solution.py:602
  182.8 59.9 %exchange_3.1 = f32[32,3,64,128]{3,2,1,0:T(8,128)} custom-call(f32[32,3,64,128]{3,2,1,0:T(8,128)} %bitcast.42), custom_call_target="tpu_custom_call" | custom-call | bytes 50331648 | tf_op jit(solution)/shard_map/exchange_3/pallas_call | solution.py:552
  242.7 0.1 broadcast_in_dim.38.keep_ref
  242.8 0.1 broadcast_in_dim.37.wave_ref
  242.8 2.2 copy-done.2
  245.0 2.2 copy-done.6
  247.2 1.9 copy-done.9
  249.1 7.1 %z_forward.2 = (f32[4,64,768]{2,1,0:T(8,128)S(1)}, f32[4,64,768]{2,1,0:T(8,128)}) custom-call(s32[1]{0:T(128)} %bitcast.half_ref, f32[8,4,3,64,128]{4,3,2,1,0:T(8,128)S(1)} %bitcast.34, bf16[8,512,512]{2,1,0:T(8,128)(2,1)S(1)} %copy-done.6, bf16[8,512,512]{2,1,0:T(8,128)(2,1)S(1)} %copy-done.2, f32[64,128]{1,0:T(8,128)S(1)} %broadcast_in_dim.37.wave_ref, ...), custom_call_target="tpu_custom_call" | custom-call | tf_op jit(solution)/shard_map/z_forward/pallas_call | solution.py:628
  256.3 2.2 collective-permute-start.2
  258.5 59.1 %exchange_4.1 = f32[32,3,64,128]{3,2,1,0:T(8,128)} custom-call(f32[32,3,64,128]{3,2,1,0:T(8,128)} %bitcast.41), custom_call_target="tpu_custom_call" | custom-call | bytes 50331648 | tf_op jit(solution)/shard_map/exchange_4/pallas_call | solution.py:552
  317.6 0.1 broadcast_in_dim.40.keep_ref
  317.6 0.1 broadcast_in_dim.39.wave_ref
  317.7 2.2 copy-done.3
  319.9 2.2 copy-done.7
  322.1 1.9 copy-done.8
  324.0 7.1 %z_forward.3 = (f32[4,64,768]{2,1,0:T(8,128)S(1)}, f32[4,64,768]{2,1,0:T(8,128)}) custom-call(s32[1]{0:T(128)} %bitcast.half_ref, f32[8,4,3,64,128]{4,3,2,1,0:T(8,128)S(1)} %bitcast.33, bf16[8,512,512]{2,1,0:T(8,128)(2,1)S(1)} %copy-done.7, bf16[8,512,512]{2,1,0:T(8,128)(2,1)S(1)} %copy-done.3, f32[64,128]{1,0:T(8,128)S(1)} %broadcast_in_dim.39.wave_ref, ...), custom_call_target="tpu_custom_call" | custom-call | tf_op jit(solution)/shard_map/z_forward/pallas_call | solution.py:628
  331.1 0.8 collective-permute-start.3
  332.6 0.0 collective-permute-done.2.refs_2_
  332.6 18.0 %collective-permute-done.3.refs_3_ = f32[4,64,768]{2,1,0:T(8,128)S(1)} collective-permute-done((f32[4,64,768]{2,1,0:T(8,128)}, f32[4,64,768]{2,1,0:T(8,128)S(1)}, u32[]{:S(2)}, u32[]{:S(2)}) %collective-permute-start.3) | collective-permute-done | bytes 786464 | tf_op jit(solution)/shard_map/ppermute | solution.py:638
  350.6 0.1 broadcast_in_dim.41.refs_4_
  350.7 8.4 %advance.1 = (f32[2,2,256,1024]{3,2,1,0:T(8,128)}, f32[2,2,256,1024]{3,2,1,0:T(8,128)}) custom-call(s32[1]{0:T(128)} %bitcast.half_ref, f32[1]{0:T(128)S(6)} %copy.13.base_ref, f32[2,2,256,1024]{3,2,1,0:T(8,128)} %bitcast.37, f32[2,2,256,1024]{3,2,1,0:T(8,128)} %bitcast.40, f32[4,64,768]{2,1,0:T(8,128)S(1)} %get-tuple-element.23.refs_0_, ...), custom_call_target="tpu_custom_call" | custom-call | tf_op jit(solution)/shard_map/advance/pallas_call | solution.py:644
  (11 shorter events, 0.1 us)
Async XLA Ops:
  4.2 24.0 %collective-permute-start = (f32[2,2,64,1024]{3,2,1,0:T(8,128)S(1)}, f32[2,2,64,1024]{3,2,1,0:T(8,128)S(1)}, u32[]{:S(2)}, u32[]{:S(2)}) collective-permute-start(f32[2,2,64,1024]{3,2,1,0:T(8,128)S(1)} %get-tuple-element.32), channel_id=1, source_target_pairs={{0,1},{1,0},{2,3},{3,2},{4,5},{5,4},{6,7},{7,6},{8,9},{9,8},{10,11... | collective-permute-start | bytes 3145736 | tf_op jit(solution)/shard_map/ppermute | solution.py:587
  28.2 1.0 copy-start.12
  29.2 63.8 %collective-permute-start.1 = (f32[2,2,64,1024]{3,2,1,0:T(8,128)}, f32[2,2,64,1024]{3,2,1,0:T(8,128)S(1)}, u32[]{:S(2)}, u32[]{:S(2)}) collective-permute-start(f32[2,2,64,1024]{3,2,1,0:T(8,128)} %get-tuple-element.19), channel_id=1, source_target_pairs={{0,1},{1,0},{2,3},{3,2},{4,5},{5,4},{6,7},{7,6},{8,9},{9,8},{10,11... | collective-permute-start | bytes 3145736 | tf_op jit(solution)/shard_map/ppermute | solution.py:587
  30.6 2.2 copy-start
  32.8 2.2 copy-start.4
  35.0 1.2 copy-start.13
  40.8 1.3 copy-start.10
  93.0 2.2 copy-start.1
  95.2 2.2 copy-start.5
  101.9 1.3 copy-start.11
  242.8 2.2 copy-start.2
  245.0 2.2 copy-start.6
  247.2 1.9 copy-start.9
  256.3 76.3 %collective-permute-start.2 = (f32[4,64,768]{2,1,0:T(8,128)}, f32[4,64,768]{2,1,0:T(8,128)S(1)}, u32[]{:S(2)}, u32[]{:S(2)}) collective-permute-start(f32[4,64,768]{2,1,0:T(8,128)} %get-tuple-element.26), channel_id=1, source_target_pairs={{0,1},{1,0},{2,3},{3,2},{4,5},{5,4},{6,7},{7,6},{8,9},{9,8},{10,11... | collective-permute-start | bytes 2359304 | tf_op jit(solution)/shard_map/ppermute | solution.py:638
  317.7 2.2 copy-start.3
  319.9 2.2 copy-start.7
  322.1 1.9 copy-start.8
  331.1 19.5 %collective-permute-start.3 = (f32[4,64,768]{2,1,0:T(8,128)}, f32[4,64,768]{2,1,0:T(8,128)S(1)}, u32[]{:S(2)}, u32[]{:S(2)}) collective-permute-start(f32[4,64,768]{2,1,0:T(8,128)} %get-tuple-element.27), channel_id=1, source_target_pairs={{0,1},{1,0},{2,3},{3,2},{4,5},{5,4},{6,7},{7,6},{8,9},{9,8},{10,11... | collective-permute-start | bytes 2359304 | tf_op jit(solution)/shard_map/ppermute | solution.py:638
